TPU v7x, 512 devices: a whole 4x4x16 slice. The times are simulated.
512 devices in a mesh: section: 2 (over x_hi), gy: 16 (over y, x_lo, core), gx: 16 (over z).
Axes of the slice: x: 4 (x_hi: 2, x_lo: 2; x = x_hi * 2 + x_lo), y: 4, z: 16, core: 2. Of those that a mesh axis runs over, the one named last changes fastest.
Arguments:
- images: bfloat16 [2, 512, 1024, 128], P('section', 'gy', 'gx'), may hold values from -6 to 6
- first_kernel: bfloat16 [3, 3, 128, 128], replicated, may hold values from -0.1875 to 0.1875
- projection: bfloat16 [128, 256], replicated, may hold values from -0.5 to 0.5
- second_kernel: bfloat16 [3, 3, 256, 256], replicated, may hold values from -0.125 to 0.125
- cotangent: bfloat16 [2, 256, 512, 256], P('section', 'gy', 'gx'), may hold values from -0.15625 to 0.15625
Outputs:
- features: bfloat16 [2, 256, 512, 256], P('section', 'gy', 'gx')
- grad_first: float32 [3, 3, 128, 128], replicated
- grad_projection: float32 [128, 256], replicated
- grad_second: float32 [3, 3, 256, 256], replicated
All inputs are finite; a program needn't handle non-finite values.
Results may differ from a plain program's by a relative error of at most 0.014.
Values may be sent and summed in bfloat16 or wider, within the bound.
A program may use at most 64 MiB of HBM per device.

v0:
```python
import jax
import jax.numpy as jnp
from jax import lax
from jax.sharding import PartitionSpec as P


def padded_2(array, sides, width):
    for axis, dim in sides:
        size, length = (lax.axis_size(axis), array.shape[dim])
        up = [(i, (i + 1) % size) for i in range(size - 1)]
        down = [(j, i) for i, j in up]
        last = lax.slice_in_dim(array, length - width, length, axis=dim)
        initial = lax.slice_in_dim(array, 0, width, axis=dim)
        before = lax.ppermute(last, axis, up)
        after = lax.ppermute(initial, axis, down)
        array = jnp.concatenate([before, array, after], axis=dim)
    return array


def from_partner(block, axis, bit):
    count = lax.axis_size(axis)
    route = []
    for low in range(count):
        high = low | 1 << bit
        if high != low and high < count:
            route += [(low, high), (high, low)]
    return lax.ppermute(block, axis, route)


def silu_slope(values):
    sigma = jax.nn.sigmoid(values)
    return sigma * (1.0 + values * (1.0 - sigma))


def conv_forward(padded, kernel, row_count, col_count):
    total = jnp.zeros((row_count * col_count, kernel.shape[3]), jnp.float32)
    for row_tap in range(3):
        for col_tap in range(3):
            piece = padded[row_tap : row_tap + row_count, col_tap : col_tap + col_count].reshape(
                row_count * col_count, padded.shape[2]
            )
            total = total + jnp.dot(
                piece, kernel[row_tap, col_tap], preferred_element_type=jnp.float32
            )
    return total


def conv_slopes(padded, slope, row_count, col_count):
    pieces = []
    for row_tap in range(3):
        for col_tap in range(3):
            piece = padded[row_tap : row_tap + row_count, col_tap : col_tap + col_count].reshape(
                row_count * col_count, padded.shape[2]
            )
            pieces.append(jnp.einsum("pc,pd->cd", piece, slope, preferred_element_type=jnp.float32))
    return jnp.stack(pieces).reshape(3, 3, padded.shape[2], slope.shape[1])


def conv_back(padded, kernel, row_count, col_count):
    total = jnp.zeros((row_count * col_count, kernel.shape[2]), jnp.float32)
    for row_tap in range(3):
        for col_tap in range(3):
            piece = padded[
                2 - row_tap : 2 - row_tap + row_count, 2 - col_tap : 2 - col_tap + col_count
            ].reshape(row_count * col_count, padded.shape[2])
            total = total + jnp.einsum(
                "pd,cd->pc", piece, kernel[row_tap, col_tap], preferred_element_type=jnp.float32
            )
    return total


def first_forward(tile, first_kernel):
    row_count, col_count, channels = tile.shape
    padded = padded_2(tile, (("gy", 0), ("gx", 1)), 1)
    before = conv_forward(padded, first_kernel, row_count, col_count)
    hidden = jax.nn.silu(before).astype(jnp.bfloat16).reshape(row_count, col_count, channels)
    pooled = (
        hidden.astype(jnp.float32)
        .reshape(row_count // 2, 2, col_count // 2, 2, channels)
        .sum(axis=(1, 3))
        * 0.25
    ).astype(jnp.bfloat16)
    return (padded, before, pooled)


def project(pooled, projection):
    half_rows, half_cols, channels = pooled.shape
    flat = jnp.dot(
        pooled.reshape(half_rows * half_cols, channels),
        projection,
        preferred_element_type=jnp.float32,
    )
    return flat.astype(jnp.bfloat16).reshape(half_rows, half_cols, projection.shape[1])


def second_pass(middle, second_kernel, upstream):
    half_rows, half_cols, wide = middle.shape
    padded = padded_2(middle, (("gy", 0), ("gx", 1)), 1)
    before = conv_forward(padded, second_kernel, half_rows, half_cols)
    output = jax.nn.silu(before).astype(jnp.bfloat16).reshape(half_rows, half_cols, wide)
    flat_up = upstream.reshape(half_rows * half_cols, wide).astype(jnp.float32)
    slope = (flat_up * silu_slope(before)).astype(jnp.bfloat16)
    kernel_grad = conv_slopes(padded, slope, half_rows, half_cols)
    slope_padded = padded_2(slope.reshape(half_rows, half_cols, wide), (("gy", 0), ("gx", 1)), 1)
    back = conv_back(slope_padded, second_kernel, half_rows, half_cols).astype(jnp.bfloat16)
    return (output, kernel_grad, back.reshape(half_rows, half_cols, wide))


def projection_back(pooled, back, projection):
    half_rows, half_cols, channels = pooled.shape
    flat_pool = pooled.reshape(half_rows * half_cols, channels)
    flat_back = back.reshape(half_rows * half_cols, back.shape[2])
    grad = jnp.einsum("pc,pd->cd", flat_pool, flat_back, preferred_element_type=jnp.float32)
    pooled_slope = jnp.einsum(
        "pd,cd->pc", flat_back, projection, preferred_element_type=jnp.float32
    )
    return (grad, pooled_slope.astype(jnp.bfloat16).reshape(half_rows, half_cols, channels))


def first_back(padded, before, pooled_slope):
    half_rows, half_cols, channels = pooled_slope.shape
    spread = jnp.broadcast_to(
        (pooled_slope.astype(jnp.float32) * 0.25)[:, None, :, None, :],
        (half_rows, 2, half_cols, 2, channels),
    )
    spread = spread.reshape(4 * half_rows * half_cols, channels)
    slope = (spread * silu_slope(before)).astype(jnp.bfloat16)
    return conv_slopes(padded, slope, 2 * half_rows, 2 * half_cols)


def per_device(images, first_kernel, projection, second_kernel, cotangent):
    padded, before, pooled = first_forward(images[0], first_kernel)
    middle = from_partner(project(pooled, projection), "section", 0)
    output, grad_second, back_far = second_pass(middle, second_kernel, cotangent[0])
    back = from_partner(back_far, "section", 0)
    grad_projection, pooled_slope = projection_back(pooled, back, projection)
    grad_first = first_back(padded, before, pooled_slope)
    grad_first, grad_projection, grad_second = lax.psum(
        (grad_first, grad_projection, grad_second), ("section", "gy", "gx")
    )
    return (output[None], grad_first, grad_projection, grad_second)


def solution(mesh):
    placed = (P("section", "gy", "gx", None), P(), P(), P(), P("section", "gy", "gx", None))
    return jax.shard_map(
        per_device,
        mesh=mesh,
        in_specs=placed,
        out_specs=(P("section", "gy", "gx", None), P(), P(), P()),
        check_vma=False,
    )
```

profile of v0, /device:TPU:2, one launch (start us, length us, event | category | flops | bytes accessed | tf_op | source)
XLA Modules:
  0.0 605.1 jit_solution(15916452577856336045)
XLA Ops:
  7.2 0.8 slice_bitcast_fusion.3
  8.0 1.9 collective-permute-start
  10.0 3.6 collective-permute-start.1
  13.6 1.4 collective-permute-done.1
  15.0 0.9 pad_maximum_fusion.15
  15.9 3.8 collective-permute-start.2
  19.8 1.4 collective-permute-start.3
  21.2 1.3 pad_maximum_fusion.1
  22.8 2.7 collective-permute-done.3
  25.6 0.3 maximum_maximum_fusion
  25.9 0.6 fusion.93
  26.5 0.3 fusion.73
  28.5 0.5 multiply_convert_fusion.1
  29.0 0.9 convert_reduce_fusion
  30.1 4.1 collective-permute-start.4
  34.3 8.2 %collective-permute-done.4 = bf16[16,32,256]{2,1,0:T(8,128)(2,1)S(1)} collective-permute-done((bf16[16,32,256]{2,1,0:T(8,128)(2,1)S(1)}, bf16[16,32,256]{2,1,0:T(8,128)(2,1)S(1)}, u32[]{:S(2)}, u32[]{:S(2)}) %collective-permute-start.4) | collective-permute-done | bytes 262176 | tf_op jit(solution)/shard_map/ppermute | solution.py:27
  42.5 2.1 collective-permute-start.5
  44.6 3.5 collective-permute-start.6
  48.1 1.4 collective-permute-done.6
  49.6 3.8 collective-permute-start.7
  53.5 1.3 collective-permute-start.8
  55.3 4.9 collective-permute-done.8
  60.1 0.4 pad_maximum_fusion.8
  61.9 0.7 copy-done.7
  62.6 1.1 fusion.26
  64.1 3.1 collective-permute-start.9
  67.2 2.5 collective-permute-start.10
  71.4 1.3 collective-permute-start.11
  72.7 6.0 collective-permute-start.12
  79.0 1.1 collective-permute-done.12
  82.7 4.0 collective-permute-start.13
  87.2 7.4 %collective-permute-done.13 = bf16[16,32,256]{2,1,0:T(8,128)(2,1)S(1)} collective-permute-done((bf16[16,32,256]{2,1,0:T(8,128)(2,1)S(1)}, bf16[16,32,256]{2,1,0:T(8,128)(2,1)S(1)}, u32[]{:S(2)}, u32[]{:S(2)}) %collective-permute-start.13) | collective-permute-done | bytes 262176 | tf_op jit(solution)/shard_map/ppermute | solution.py:27
  94.9 0.5 broadcast_in_dim.2
  95.4 0.4 multiply_convert_fusion
  95.8 0.3 fusion.25
  96.1 0.4 fusion.24
  96.5 0.4 fusion.23
  96.9 0.4 fusion.22
  97.2 0.4 fusion.21
  97.6 0.4 fusion.20
  97.9 0.4 fusion.19
  98.3 0.4 fusion.18
  98.7 0.4 fusion.17
  99.0 0.9 convolution_bitcast_fusion.9
  99.9 492.5 %all-reduce.3.cloned.1.call-done = (f32[3,3,128,128]{3,2,1,0:T(8,128)}, f32[128,256]{1,0:T(8,128)}, f32[3,3,256,256]{3,2,1,0:T(8,128)}) async-done(((f32[3,3,128,128]{3,2,1,0:T(8,128)}, f32[128,256]{1,0:T(8,128)}, f32[3,3,256,256]{3,2,1,0:T(8,128)}), (f32[3,3,128,128]{3,2,1,0:T(8,128)}, f32[128,256]{1,0:T(8,128)}, f32[3,3,256,256]{3,2,1,0:T(8,128)})) %all-reduce.3.cloned.1.call-update) | async-done | bytes 3080208 | tf_op jit(solution)/shard_map/psum | solution.py:138
  592.4 2.0 copy.32
  594.4 0.7 copy.33
  595.0 3.2 copy.34
  (71 shorter events, 9.7 us)
Async XLA Ops:
  7.2 22.7 %copy-start = (bf16[128,256]{1,0:T(8,128)(2,1)S(1)}, bf16[128,256]{1,0:T(8,128)(2,1)}, u32[]{:S(2)}) copy-start(bf16[128,256]{1,0:T(8,128)(2,1)} %param.7) | copy-start | bytes 196612
  7.2 15.3 %copy-start.5 = (bf16[3,3,128,128]{3,2,1,0:T(8,128)(2,1)S(1)}, bf16[3,3,128,128]{3,2,1,0:T(8,128)(2,1)}, u32[]{:S(2)}) copy-start(bf16[3,3,128,128]{3,2,1,0:T(8,128)(2,1)} %param.6) | copy-start | bytes 884740
  7.2 585.2 %all-reduce.3.cloned.1.call-start = ((), (), s32[]{:S(2)}) async-start(), calls=%async_computation | async-start | bytes 6160384 | tf_op jit(solution)/shard_map/psum | solution.py:138
  8.0 5.6 collective-permute-start
  10.0 5.1 collective-permute-start.1
  15.9 6.9 %collective-permute-start.2 = (bf16[34,1,128]{2,1,0:T(2,128)(2,1)S(1)}, bf16[34,1,128]{2,1,0:T(2,128)(2,1)S(1)}, u32[]{:S(2)}, u32[]{:S(2)}) collective-permute-start(bf16[34,1,128]{2,1,0:T(2,128)(2,1)S(1)} %get-tuple-element.15), channel_id=1, source_target_pairs={{0,1},{1,2},{2,3},{3,4},{4,5},{5,6},{6,7},{7,8},{8,9},{9,10},{10,1... | collective-permute-start | bytes 26120 | tf_op jit(solution)/shard_map/ppermute | solution.py:14
  19.8 5.8 copy-start.1
  19.8 5.8 collective-permute-start.3
  29.9 24.9 %copy-start.2 = (bf16[3,3,256,256]{3,2,1,0:T(8,128)(2,1)S(1)}, bf16[3,3,256,256]{3,2,1,0:T(8,128)(2,1)}, u32[]{:S(2)}) copy-start(bf16[3,3,256,256]{3,2,1,0:T(8,128)(2,1)} %param.8) | copy-start | bytes 3538948
  30.1 12.4 %collective-permute-start.4 = (bf16[16,32,256]{2,1,0:T(8,128)(2,1)S(1)}, bf16[16,32,256]{2,1,0:T(8,128)(2,1)S(1)}, u32[]{:S(2)}, u32[]{:S(2)}) collective-permute-start(bf16[16,32,256]{2,1,0:T(8,128)(2,1)S(1)} %bitcast.328), channel_id=1, source_target_pairs={{0,256},{256,0},{1,257},{257,1},{2,258},{258,2},{3,259},{259,3},{4... | collective-permute-start | bytes 786440 | tf_op jit(solution)/shard_map/ppermute | solution.py:27
  42.5 5.6 collective-permute-start.5
  44.6 4.9 collective-permute-start.6
  49.6 5.6 collective-permute-start.7
  53.5 6.7 %collective-permute-start.8 = (bf16[18,1,256]{2,1,0:T(2,128)(2,1)S(1)}, bf16[18,1,256]{2,1,0:T(2,128)(2,1)S(1)}, u32[]{:S(2)}, u32[]{:S(2)}) collective-permute-start(bf16[18,1,256]{2,1,0:T(2,128)(2,1)S(1)} %get-tuple-element.43), channel_id=1, source_target_pairs={{1,0},{2,1},{3,2},{4,3},{5,4},{6,5},{7,6},{8,7},{9,8},{10,9},{11,1... | collective-permute-start | bytes 27656 | tf_op jit(solution)/shard_map/ppermute | solution.py:15
  61.7 1.0 copy-start.7
  64.1 7.3 %collective-permute-start.9 = (bf16[1,32,256]{2,1,0:T(8,128)(2,1)S(1)}, bf16[1,32,256]{2,1,0:T(8,128)(2,1)S(1)}, u32[]{:S(2)}, u32[]{:S(2)}) collective-permute-start(bf16[1,32,256]{2,1,0:T(8,128)(2,1)S(1)} %get-tuple-element.46), channel_id=1, source_target_pairs={{0,16},{16,32},{32,48},{48,64},{64,80},{80,96},{96,112},{112,128},... | collective-permute-start | bytes 49160 | tf_op jit(solution)/shard_map/ppermute | solution.py:14
  67.2 4.2 collective-permute-start.10
  71.4 7.6 %collective-permute-start.11 = (bf16[18,1,256]{2,1,0:T(2,128)(2,1)S(1)}, bf16[18,1,256]{2,1,0:T(2,128)(2,1)S(1)}, u32[]{:S(2)}, u32[]{:S(2)}) collective-permute-start(bf16[18,1,256]{2,1,0:T(2,128)(2,1)S(1)} %get-tuple-element.37), channel_id=1, source_target_pairs={{1,0},{2,1},{3,2},{4,3},{5,4},{6,5},{7,6},{8,7},{9,8},{10,9},{11,1... | collective-permute-start | bytes 27656 | tf_op jit(solution)/shard_map/ppermute | solution.py:15
  72.7 7.4 %collective-permute-start.12 = (bf16[18,1,256]{2,1,0:T(2,128)(2,1)S(1)}, bf16[18,1,256]{2,1,0:T(2,128)(2,1)S(1)}, u32[]{:S(2)}, u32[]{:S(2)}) collective-permute-start(bf16[18,1,256]{2,1,0:T(2,128)(2,1)S(1)} %get-tuple-element.38), channel_id=1, source_target_pairs={{0,1},{1,2},{2,3},{3,4},{4,5},{5,6},{6,7},{7,8},{8,9},{9,10},{10,1... | collective-permute-start | bytes 27656 | tf_op jit(solution)/shard_map/ppermute | solution.py:14
  82.7 12.0 %collective-permute-start.13 = (bf16[16,32,256]{2,1,0:T(8,128)(2,1)S(1)}, bf16[16,32,256]{2,1,0:T(8,128)(2,1)S(1)}, u32[]{:S(2)}, u32[]{:S(2)}) collective-permute-start(bf16[16,32,256]{2,1,0:T(8,128)(2,1)S(1)} %bitcast.329), channel_id=1, source_target_pairs={{0,256},{256,0},{1,257},{257,1},{2,258},{258,2},{3,259},{259,3},{4... | collective-permute-start | bytes 786440 | tf_op jit(solution)/shard_map/ppermute | solution.py:27
  87.2 8.6 %copy-start.3 = (f32[9,256,256]{2,1,0:T(8,128)}, f32[9,256,256]{2,1,0:T(8,128)S(1)}, u32[]{:S(2)}) copy-start(f32[9,256,256]{2,1,0:T(8,128)S(1)} %fusion.6) | copy-start | bytes 7077892
  99.0 0.9 copy-start.4
  592.4 2.0 copy-start.6
Sparse Core Ops, SparseCore 0:
  100.1 492.3 all-reduce.2
where the time goes:
time: 606 us; the launch traced here: 605 us
  waiting for transfers between devices  520 us (86%)
  starting transfers between devices  42.4 us (7%)
  matrix products  14.9 us (2%)
  between operations  14.7 us (2%)
  local copies, waits for them, and re-layouts  8.72 us (1%)
    psum x1, waiting for transfers between devices, per_device(): lax.psum((grad_first, grad_projection, grad_second), ('section', 'gy', 'g...  492 us
    ppermute x6, starting transfers between devices, padded_2(): before = lax.ppermute(last, axis, up)  20.7 us
    ppermute x2, waiting for transfers between devices, from_partner(): return lax.ppermute(block, axis, route)  15.7 us
    ppermute x6, starting transfers between devices, padded_2(): after = lax.ppermute(initial, axis, down)  13.6 us
  transfers between devices with their start and end apart: 15, of which 8 were waited for; matrix products, arithmetic and copies ran while one was open for 1% of the time, Pallas kernels for 0%

commit v1 on v0

--- a/solution.py
+++ b/solution.py
@@ -136,7 +136,8 @@
     grad_projection, pooled_slope = projection_back(pooled, back, projection)
     grad_first = first_back(padded, before, pooled_slope)
     grad_first, grad_projection, grad_second = lax.psum(
-        (grad_first, grad_projection, grad_second), ("section", "gy", "gx")
+        lax.psum((grad_first, grad_projection, grad_second), axis_name="section"),
+        axis_name=("gy", "gx"),
     )
     return (output[None], grad_first, grad_projection, grad_second)
 

time: 606 us -> 2320 us (3.83)
  the two profiles are of different devices: /device:TPU:2 before, /device:TPU:4 now
where the time goes in v1:
time: 2320 us; the launch traced here: 2310 us
  waiting for transfers between devices  2240 us (97%)
  starting transfers between devices  35.8 us (2%)
    psum x1, waiting for transfers between devices, per_device(): lax.psum(lax.psum((grad_first, grad_projection, grad_second), axis_name='...  2090 us
    psum x1, waiting for transfers between devices, per_device(): lax.psum((grad_first, grad_projection, grad_second), axis_name='section')  113 us
  transfers between devices with their start and end apart: 16, of which 10 were waited for; matrix products, arithmetic and copies ran while one was open for 0% of the time, Pallas kernels for 0%

profile of v1, /device:TPU:4, one launch (start us, length us, event | category | flops | bytes accessed | tf_op | source)
XLA Modules:
  0.0 2314.4 jit_solution(2782414319264625042)
XLA Ops:
  7.2 0.8 slice_bitcast_fusion.3
  8.0 1.7 collective-permute-start
  9.8 1.3 collective-permute-start.1
  11.1 2.8 collective-permute-done.1
  13.8 0.9 pad_maximum_fusion.15
  14.7 3.8 collective-permute-start.2
  18.6 1.4 collective-permute-start.3
  20.0 1.3 pad_maximum_fusion.1
  21.6 2.7 collective-permute-done.3
  24.7 0.6 fusion.93
  27.3 0.5 multiply_convert_fusion.1
  27.8 0.9 convert_reduce_fusion
  28.9 4.0 collective-permute-start.4
  32.9 8.4 collective-permute-done.4
  41.3 2.0 collective-permute-start.5
  43.4 1.3 collective-permute-start.6
  44.7 3.4 collective-permute-done.6
  48.2 3.8 collective-permute-start.7
  52.0 1.3 collective-permute-start.8
  53.8 4.8 collective-permute-done.8
  58.6 0.4 pad_maximum_fusion.8
  60.4 0.7 copy-done.7
  61.1 1.1 fusion.26
  62.6 3.2 collective-permute-start.9
  65.8 1.3 collective-permute-start.10
  68.8 0.7 collective-permute-done.10
  69.6 1.3 collective-permute-start.11
  70.9 6.1 collective-permute-start.12
  77.3 1.1 collective-permute-done.12
  81.0 3.1 collective-permute-start.13
  84.7 8.3 collective-permute-done.13
  93.2 0.5 broadcast_in_dim.2
  93.7 0.4 multiply_convert_fusion
  94.1 0.4 fusion.25
  94.5 0.4 fusion.24
  94.8 0.4 fusion.23
  95.2 0.4 fusion.22
  95.6 0.4 fusion.21
  95.9 0.4 fusion.20
  96.3 0.4 fusion.19
  96.6 0.4 fusion.18
  97.0 0.4 fusion.17
  97.4 0.9 convolution_bitcast_fusion.9
  98.3 112.7 %all-reduce.7.cloned.1.call-done = (f32[3,3,128,128]{3,2,1,0:T(8,128)}, f32[128,256]{1,0:T(8,128)}, f32[3,3,256,256]{3,2,1,0:T(8,128)}) async-done(((f32[3,3,128,128]{3,2,1,0:T(8,128)}, f32[128,256]{1,0:T(8,128)}, f32[3,3,256,256]{3,2,1,0:T(8,128)}), (f32[3,3,128,128]{3,2,1,0:T(8,128)}, f32[128,256]{1,0:T(8,128)}, f32[3,3,256,256]{3,2,1,0:T(8,128)})) %all-reduce.7.cloned.1.call-update) | async-done | bytes 3080208 | tf_op jit(solution)/shard_map/psum | solution.py:139
  211.0 2090.7 %all-reduce.5.cloned.1.call-done = (f32[3,3,128,128]{3,2,1,0:T(8,128)}, f32[128,256]{1,0:T(8,128)}, f32[3,3,256,256]{3,2,1,0:T(8,128)}) async-done(((f32[3,3,128,128]{3,2,1,0:T(8,128)}, f32[128,256]{1,0:T(8,128)}, f32[3,3,256,256]{3,2,1,0:T(8,128)}), (f32[3,3,128,128]{3,2,1,0:T(8,128)}, f32[128,256]{1,0:T(8,128)}, f32[3,3,256,256]{3,2,1,0:T(8,128)})) %all-reduce.5.cloned.1.call-update) | async-done | bytes 3080208 | tf_op jit(solution)/shard_map/psum | solution.py:138
  2301.8 2.0 copy.35
  2303.7 0.7 copy.36
  2304.4 3.2 copy.37
  (74 shorter events, 10.4 us)
Async XLA Ops:
  7.2 21.5 copy-start
  7.2 14.1 copy-start.5
  7.2 203.8 %all-reduce.7.cloned.1.call-start = ((), (), s32[]{:S(2)}) async-start(), calls=%async_computation.1 | async-start | bytes 6160384 | tf_op jit(solution)/shard_map/psum | solution.py:139
  8.0 3.0 collective-permute-start
  9.8 4.1 collective-permute-start.1
  14.7 6.9 collective-permute-start.2
  18.6 5.8 copy-start.1
  18.6 5.8 collective-permute-start.3
  28.6 24.7 %copy-start.2 = (bf16[3,3,256,256]{3,2,1,0:T(8,128)(2,1)S(1)}, bf16[3,3,256,256]{3,2,1,0:T(8,128)(2,1)}, u32[]{:S(2)}) copy-start(bf16[3,3,256,256]{3,2,1,0:T(8,128)(2,1)} %param.8) | copy-start | bytes 3538948
  28.9 12.4 collective-permute-start.4
  41.3 3.3 collective-permute-start.5
  43.4 4.7 collective-permute-start.6
  48.2 5.6 collective-permute-start.7
  52.0 6.6 collective-permute-start.8
  60.2 1.0 copy-start.7
  62.6 6.2 collective-permute-start.9
  65.8 3.7 collective-permute-start.10
  69.6 7.7 collective-permute-start.11
  70.9 7.5 collective-permute-start.12
  81.0 12.0 collective-permute-start.13
  84.7 9.4 copy-start.3
  97.3 0.9 copy-start.4
  98.3 2203.5 %all-reduce.5.cloned.1.call-start = ((), (), s32[]{:S(2)}) async-start(), calls=%async_computation | async-start | bytes 6160384 | tf_op jit(solution)/shard_map/psum | solution.py:138
  2301.8 2.0 copy-start.6
Sparse Core Ops, SparseCore 0:
  98.4 112.5 all-reduce.6
  214.4 2087.2 all-reduce.4
